TPU v7x, 256 devices: a whole 4x4x8 slice. The times are simulated.
256 devices in a mesh: learn: 8 (over z_lo, x), expert: 32 (over z_hi, y, core).
Axes of the slice: x: 4, y: 4, z: 8 (z_hi: 4, z_lo: 2; z = z_hi * 2 + z_lo), core: 2. Of those that a mesh axis runs over, the one named last changes fastest.
Arguments:
- update: float32 [32, 160, 128, 128], P('learn', 'expert'), may hold values from -3 to 3
- resident: bfloat16 [32, 2560, 1024], P('expert'), may hold values from -6 to 6
- placement: int32 [32], replicated, may hold values from 0 to 31, each once
- counts: int32 [32], replicated, may hold values from 1 to 160, as said below
Outputs:
- refreshed: bfloat16 [32, 2560, 1024], P('expert')
Inputs may be any that keep to these rules, and one draw needn't show every extreme that they name: `counts`: some expert changes all 160 blocks and another exactly one.
All inputs are finite; a program needn't handle non-finite values.
Results may differ from a plain program's by a relative error of at most 0.0034.
Values may be sent and summed in bfloat16 or wider, within the bound.
A program may use at most 128 MiB of HBM per device.

v0:
```python
import jax
import jax.numpy as jnp
from jax import lax
from jax.sharding import PartitionSpec as P


def apply_delta(resident, code_block, scale_block, changed_count):
    tile_total = code_block.shape[0]
    tile_side = code_block.shape[2]
    row_count = resident.shape[1]
    col_count = resident.shape[2]
    changed = (jnp.arange(tile_total, dtype=jnp.int32) < changed_count).astype(jnp.float32)
    decoded = (
        code_block.astype(jnp.float32) * (scale_block.astype(jnp.float32) * changed)[:, None, None]
    )
    window = decoded.reshape(row_count // tile_side, col_count // tile_side, tile_side, tile_side)
    window = window.transpose(0, 2, 1, 3).reshape(row_count, col_count)
    return (resident[0].astype(jnp.float32) + window).astype(jnp.bfloat16)[None]


def on_device(update, resident, placement, counts):
    largest = jnp.max(jnp.abs(update), axis=(2, 3))
    block_scale = ((largest + 1e-06) / 448.0).astype(jnp.bfloat16)
    code_tiles = (update / block_scale.astype(jnp.float32)[:, :, None, None]).astype(jnp.bfloat16)
    expert_total = placement.shape[0]
    slot_ids = jnp.arange(expert_total, dtype=jnp.int32)
    owner_expert = jnp.sum(
        jnp.where(placement[None, :] == slot_ids[:, None], slot_ids[None, :], 0), axis=1
    )
    held_expert = owner_expert[lax.axis_index("expert")]
    gathered_codes, gathered_scales = (
        lax.all_gather(code_tiles, "learn", axis=0, tiled=True),
        lax.all_gather(block_scale, "learn", axis=0, tiled=True),
    )
    ordered_codes = jnp.take(gathered_codes, owner_expert, axis=0)
    ordered_scales = jnp.take(gathered_scales, owner_expert, axis=0)
    received_codes, received_scales = (
        lax.all_to_all(ordered_codes, "expert", split_axis=0, concat_axis=1, tiled=True),
        lax.all_to_all(ordered_scales, "expert", split_axis=0, concat_axis=1, tiled=True),
    )
    refreshed = apply_delta(resident, received_codes[0], received_scales[0], counts[held_expert])
    return refreshed


def solution(mesh):
    placed = (P("learn", "expert", None, None), P("expert", None, None), P(), P())
    return jax.shard_map(
        on_device, mesh=mesh, in_specs=placed, out_specs=P("expert", None, None), check_vma=False
    )
```

profile of v0, /device:TPU:1, one launch (start us, length us, event | category | flops | bytes accessed | tf_op | source)
XLA Modules:
  0.0 263.9 jit_solution(16183287349164211104)
XLA Ops:
  6.5 0.0 all-gather.3.cloned.1.call-start
  6.5 1.5 abs_reduce_fusion
  8.1 2.4 divide_convert_fusion
  10.4 0.0 all-gather.3.cloned.1.call-update
  10.5 16.4 %all-gather = bf16[8,4,5]{2,1,0:T(4,128)(2,1)S(1)} all-gather(bf16[1,4,5]{2,1,0:T(4,128)(2,1)S(1)} %get-tuple-element.5), channel_id=1, replica_groups=mesh['learn'=8,'expert'=32] {'learn'}, dimensions={0}, use_global_device_ids=true | all-gather | bytes 360 | tf_op jit(solution)/shard_map/all_gather | solution.py:33
  26.9 0.8 select_reduce_fusion
  27.6 0.6 gather_fusion.1
  28.3 0.1 bitcast_select_fusion
  28.3 0.6 copy.9
  28.9 14.7 %all-to-all-start.1 = ((bf16[32,1,5]{2,1,0:T(2,128)(2,1)}), bf16[32,1,5]{2,1,0:T(2,128)(2,1)S(1)}, u32[]{:S(2)}, u32[]{:S(2)}) async-start(bf16[32,1,5]{2,1,0:T(2,128)(2,1)} %copy.9), calls=%async_computation.1 | async-start | bytes 32768 | tf_op jit(solution)/shard_map/all_to_all | solution.py:39
  43.6 36.2 %all-gather.3.cloned.1.call-done = bf16[32,5,128,128]{3,2,1,0:T(8,128)(2,1)} async-done(((bf16[4,5,128,128]{3,2,1,0:T(8,128)(2,1)}), bf16[32,5,128,128]{3,2,1,0:T(8,128)(2,1)}) %all-gather.3.cloned.1.call-update) | async-done | bytes 5242896 | tf_op jit(solution)/shard_map/all_gather | solution.py:32
  79.8 6.1 %gather_fusion = bf16[32,5,128,128]{3,2,1,0:T(8,128)(2,1)} fusion(bf16[32,5,128,128]{3,2,1,0:T(8,128)(2,1)} %all-gather.3.cloned.1.call-done, s32[1024]{0:T(1024)S(1)} %pad_clamp_fusion), kind=kCustom, calls=%fused_computation | custom fusion | bytes 10485888 | tf_op jit(solution)/shard_map/jit(_take)/gather | solution.py:35
  85.9 5.4 %broadcast_select_fusion = bf16[32,5,128,128]{3,2,1,0:T(8,128)(2,1)} fusion(bf16[32,5,128,128]{3,2,1,0:T(8,128)(2,1)} %gather_fusion, pred[32]{0:T(512)(128)(4,1)S(1)} %compare_and_fusion), kind=kLoop, calls=%fused_computation.5 | loop fusion | flops 2621440 | bytes 10485792 | tf_op jit(solution)/shard_map/jit(_take)/select_n | solution.py:35
  91.3 0.0 copy-start
  91.3 0.0 all-to-all-done.1
  91.3 9.6 %all-to-all-start = ((bf16[32,5,128,128]{3,2,1,0:T(8,128)(2,1)}), bf16[32,5,128,128]{3,2,1,0:T(8,128)(2,1)}, u32[]{:S(2)}, u32[]{:S(2)}) async-start(bf16[32,5,128,128]{3,2,1,0:T(8,128)(2,1)} %broadcast_select_fusion), calls=%async_computation | async-start | bytes 10485760 | tf_op jit(solution)/shard_map/all_to_all | solution.py:38
  100.9 0.7 dynamic_slice.6
  103.4 0.0 copy-done
  103.4 0.7 dynamic_slice.7
  104.1 0.1 convert_reduce_fusion
  104.2 0.1 reshape.83
  104.2 0.6 fusion.1
  104.9 115.0 %all-to-all-done = bf16[32,5,128,128]{3,2,1,0:T(8,128)(2,1)} async-done(((bf16[32,5,128,128]{3,2,1,0:T(8,128)(2,1)}), bf16[32,5,128,128]{3,2,1,0:T(8,128)(2,1)}, u32[]{:S(2)}, u32[]{:S(2)}) %all-to-all-start) | async-done | bytes 5242912 | tf_op jit(solution)/shard_map/all_to_all | solution.py:38
  219.9 3.2 %fusion = f32[20,128,8,128]{3,1,2,0:T(8,128)S(1)} fusion(bf16[20,8,128,128]{3,2,1,0:T(8,128)(2,1)} %bitcast.9, f32[20,8]{1,0:T(8,128)S(1)} %fusion.1), kind=kLoop, calls=%fused_computation.3 | loop fusion | flops 5242880 | bytes 15729280 | tf_op jit(solution)/shard_map/transpose | solution.py:17
  223.1 12.7 %copy.10 = f32[20,128,8,128]{3,2,1,0:T(8,128)} copy(f32[20,128,8,128]{3,1,2,0:T(8,128)S(1)} %fusion) | data formatting | bytes 20971520 | tf_op jit(solution)/shard_map/transpose | solution.py:17
  235.8 11.4 %reshape.81 = f32[1,2560,1024]{2,1,0:T(8,128)} reshape(f32[20,128,8,128]{3,2,1,0:T(8,128)} %copy.10) | data formatting | bytes 20971520 | tf_op jit(solution)/shard_map/reshape | solution.py:17
  247.3 9.8 %add_convert_fusion = bf16[1,2560,1024]{2,1,0:T(8,128)(2,1)} fusion(f32[1,2560,1024]{2,1,0:T(8,128)} %reshape.81, bf16[1,2560,1024]{2,1,0:T(8,128)(2,1)} %param.5), kind=kLoop, calls=%fused_computation.4 | loop fusion | flops 7864320 | bytes 20971520 | tf_op jit(solution)/shard_map/convert_element_type | solution.py:18
  (4 shorter events, 0.0 us)
Async XLA Ops:
  6.5 73.3 %all-gather.3.cloned.1.call-start = ((), (), s32[]{:S(2)}) async-start(), calls=%async_computation.2 | async-start | bytes 5898240 | tf_op jit(solution)/shard_map/all_gather | solution.py:32
  28.9 62.3 %all-to-all-start.1 = ((bf16[32,1,5]{2,1,0:T(2,128)(2,1)}), bf16[32,1,5]{2,1,0:T(2,128)(2,1)S(1)}, u32[]{:S(2)}, u32[]{:S(2)}) async-start(bf16[32,1,5]{2,1,0:T(2,128)(2,1)} %copy.9), calls=%async_computation.1 | async-start | bytes 32768 | tf_op jit(solution)/shard_map/all_to_all | solution.py:39
  91.3 12.2 %copy-start = (s32[32]{0:T(128)S(1)}, s32[32]{0:T(128)}, u32[]{:S(2)}) copy-start(s32[32]{0:T(128)} %param.7) | copy-start | bytes 388
  91.3 128.6 %all-to-all-start = ((bf16[32,5,128,128]{3,2,1,0:T(8,128)(2,1)}), bf16[32,5,128,128]{3,2,1,0:T(8,128)(2,1)}, u32[]{:S(2)}, u32[]{:S(2)}) async-start(bf16[32,5,128,128]{3,2,1,0:T(8,128)(2,1)} %broadcast_select_fusion), calls=%async_computation | async-start | bytes 10485760 | tf_op jit(solution)/shard_map/all_to_all | solution.py:38
Sparse Core Ops, SparseCore 0:
  10.6 69.1 all-gather.2
where the time goes:
time: 265 us; the launch traced here: 264 us
  waiting for transfers between devices  151 us (57%)
  local copies, waits for them, and re-layouts  32.8 us (12%)
  starting transfers between devices  24.3 us (9%)
  other arithmetic  23.9 us (9%)
  blocking collectives  16.4 us (6%)
  between operations  15.4 us (6%)
    all_to_all x1, waiting for transfers between devices, on_device(): lax.all_to_all(ordered_codes, 'expert', split_axis=0, concat_axis=1, tile...  115 us
    all_gather x1, waiting for transfers between devices, on_device(): lax.all_gather(code_tiles, 'learn', axis=0, tiled=True)  36.2 us
    all_gather x1, blocking collectives, on_device(): lax.all_gather(block_scale, 'learn', axis=0, tiled=True)  16.4 us
    all_to_all x1, starting transfers between devices, on_device(): lax.all_to_all(ordered_scales, 'expert', split_axis=0, concat_axis=1, til...  14.7 us
    transpose x1, local copies, waits for them, and re-layouts, apply_delta(): window = window.transpose(0, 2, 1, 3).reshape(row_count, col_count)  12.7 us
    reshape x1, local copies, waits for them, and re-layouts, apply_delta(): window = window.transpose(0, 2, 1, 3).reshape(row_count, col_count)  11.4 us
    convert_element_type x1, other arithmetic, apply_delta(): return (resident[0].astype(jnp.float32) + window).astype(jnp.bfloat16)[None]  9.82 us
    all_to_all x1, starting transfers between devices, on_device(): lax.all_to_all(ordered_codes, 'expert', split_axis=0, concat_axis=1, tile...  9.58 us
  transfers between devices with their start and end apart: 3, of which 2 were waited for; matrix products, arithmetic and copies ran while one was open for 6% of the time, Pallas kernels for 0%

commit v1 on v0

v1 whole, which is shorter than its diff:
```python
import jax
import jax.numpy as jnp
from jax import lax
from jax.experimental import pallas as pl
from jax.experimental.pallas import tpu as pltpu
from jax.sharding import PartitionSpec as P

MESH = pl.DeviceIdType.MESH
NX, NZ, NH, NY, NC = 4, 2, 4, 4, 2
NL, NE = 8, 32
EXP, PER, TPD = 4, 8, 5
SLAB, LANE = 16, 128
BLK = 40
ROW_TILES = 5


def kernel(update, resident, placement, counts, out,
           upd, res, acc, s1, r1, s2, gat, owner,
           upd_sem, res_sem, out_sem, s1_send, s1_recv, s2_send, s2_recv,
           g_send, g_recv):
    l = lax.axis_index("learn")
    e = lax.axis_index("expert")
    zl, x = l // NX, l % NX
    zh, y, c = e // (NY * NC), (e // NC) % NY, e % NC
    right = (zl * NX + (x + 1) % NX, e)
    left = (zl * NX + (x + 3) % NX, e)
    across = ((1 - zl) * NX + x, e)

    upd_in = pltpu.make_async_copy(update, upd, upd_sem)
    upd_in.start()
    res_in = pltpu.make_async_copy(resident, res, res_sem)
    res_in.start()

    learn_peers = [(((zl + dz) % NZ) * NX + (x + dx) % NX) for dz in range(NZ) for dx in range(NX) if (dz, dx) != (0, 0)]

    def slot(dh, dy, dc):
        return ((zh + dh) % NH) * (NY * NC) + ((y + dy) % NY) * NC + (c + dc) % NC

    near = [slot(0, dy, dc) for dy in range(NY) for dc in range(NC) if (dy, dc) != (0, 0)]
    far = {dh: [slot(dh, dy, dc) for dy in range(NY) for dc in range(NC)] for dh in (1, 3, 2)}
    expert_peers = near + far[1] + far[3] + far[2]

    barrier = pltpu.get_barrier_semaphore()
    for peer in learn_peers:
        pl.semaphore_signal(barrier, inc=1, device_id=(peer, e), device_id_type=MESH)
    for peer in expert_peers:
        pl.semaphore_signal(barrier, inc=1, device_id=(l, peer), device_id_type=MESH)

    upd_in.wait()

    def encode(t, carry):
        i = t // TPD
        j = t % TPD
        u = upd[t]
        largest = jnp.max(jnp.abs(u), axis=(0, 1), keepdims=True)
        scale = ((largest + 1e-06) / 448.0).astype(jnp.bfloat16).astype(jnp.float32)
        code = (u / scale).astype(jnp.bfloat16).astype(jnp.float32)
        changed = jnp.where(e * TPD + j < counts[l * EXP + i], 1.0, 0.0).astype(jnp.float32)
        s1[:, t] = (code * (scale * changed)).astype(jnp.bfloat16).reshape(NL, SLAB, LANE)
        return carry

    lax.fori_loop(0, EXP * TPD, encode, 0)
    pl.semaphore_wait(barrier, len(learn_peers) + len(expert_peers))

    sends1 = []
    for n, peer in enumerate(learn_peers):
        cp = pltpu.make_async_remote_copy(
            src_ref=s1.at[peer], dst_ref=r1.at[l], send_sem=s1_send.at[n], recv_sem=s1_recv.at[l],
            device_id=(peer, e), device_id_type=MESH)
        cp.start()
        sends1.append(cp)
    r1[l] = s1[l]

    def owner_of(k, carry):
        def add(n, total):
            return jnp.maximum(total, jnp.where(placement[n] == k, n, 0))
        owner[k] = lax.fori_loop(0, NE, add, 0, unroll=True)
        return carry

    lax.fori_loop(0, NE, owner_of, 0)

    def recv1(peer):
        return pltpu.make_async_remote_copy(
            src_ref=r1.at[peer], dst_ref=r1.at[peer], send_sem=s1_send.at[0], recv_sem=s1_recv.at[peer],
            device_id=(peer, e), device_id_type=MESH)

    for peer in learn_peers:
        recv1(peer).wait_recv()

    def picked(k):
        o = owner[k]
        return r1[o // EXP, pl.ds((o % EXP) * TPD, TPD)]

    sends2 = []
    for n, k in enumerate(expert_peers):
        s2[n] = picked(k)
        cp = pltpu.make_async_remote_copy(
            src_ref=s2.at[n], dst_ref=gat.at[l, zh, pl.ds((y * NC + c) * TPD, TPD)],
            send_sem=s2_send.at[n], recv_sem=s2_recv.at[e],
            device_id=(l, k), device_id_type=MESH)
        cp.start()
        sends2.append(cp)
    gat[l, zh, pl.ds((y * NC + c) * TPD, TPD)] = picked(e)

    def recv2(k):
        ref = gat.at[l, k // (NY * NC), pl.ds((k % (NY * NC)) * TPD, TPD)]
        pltpu.make_async_remote_copy(
            src_ref=ref, dst_ref=ref, send_sem=s2_send.at[0], recv_sem=s2_recv.at[k],
            device_id=(l, k), device_id_type=MESH).wait_recv()

    sends3 = []

    def plane(dz, dx):
        return ((zl + dz) % NZ) * NX + (x + dx) % NX

    def part(src, q, half):
        if half is None:
            return gat.at[src, q]
        return gat.at[src, q, pl.ds(half * (BLK // 2), BLK // 2)]

    def push(src, q, to, half=None):
        ref = part(src, q, half)
        cp = pltpu.make_async_remote_copy(
            src_ref=ref, dst_ref=ref, send_sem=g_send.at[len(sends3)], recv_sem=g_recv.at[src, q, 0 if half is None else half],
            device_id=to, device_id_type=MESH)
        cp.start()
        sends3.append(cp)

    def arrive(src, q, half=None):
        ref = part(src, q, half)
        pltpu.make_async_remote_copy(
            src_ref=ref, dst_ref=ref, send_sem=g_send.at[0], recv_sem=g_recv.at[src, q, 0 if half is None else half],
            device_id=across, device_id_type=MESH).wait_recv()

    def add(src, q):
        def row(a, carry):
            at = pl.multiple_of((q * ROW_TILES + a) * LANE + src * SLAB, SLAB)
            for b in range(8):
                cols = pl.ds(b * LANE, LANE)
                acc[pl.ds(at, SLAB), cols] = (
                    res[pl.ds(at, SLAB), cols].astype(jnp.float32) + gat[src, q, a * 8 + b].astype(jnp.float32)
                ).astype(jnp.bfloat16)
            return carry
        lax.fori_loop(0, ROW_TILES, row, 0)

    chunk = {dh: (zh + dh) % NH for dh in range(NH)}
    own = plane(0, 0)

    for k in near:
        recv2(k)
    q0 = chunk[0]
    push(own, q0, right)
    push(own, q0, left)
    res_in.wait()
    add(own, q0)
    arrive(plane(0, 3), q0)
    push(plane(0, 3), q0, right, 0)
    arrive(plane(0, 1), q0)
    push(plane(0, 1), q0, left, 1)
    add(plane(0, 3), q0)
    add(plane(0, 1), q0)

    rest = (1, 3, 2)
    for dh in rest:
        q = chunk[dh]
        for k in far[dh]:
            recv2(k)
        push(own, q, across)
        push(own, q, right)
        push(own, q, left)
        add(own, q)
    arrive(plane(0, 2), q0, 0)
    arrive(plane(0, 2), q0, 1)
    add(plane(0, 2), q0)
    for dx in range(NX):
        push(plane(0, dx), q0, across)
    for dh in rest:
        q = chunk[dh]
        arrive(plane(0, 3), q)
        push(plane(0, 3), q, right, 0)
        arrive(plane(0, 1), q)
        push(plane(0, 1), q, left, 1)
        arrive(plane(1, 0), q)
        push(plane(1, 0), q, right)
        push(plane(1, 0), q, left)
        add(plane(0, 3), q)
        add(plane(0, 1), q)
        add(plane(1, 0), q)
    for dh in rest:
        q = chunk[dh]
        arrive(plane(0, 2), q, 0)
        arrive(plane(0, 2), q, 1)
        add(plane(0, 2), q)
        arrive(plane(1, 3), q)
        push(plane(1, 3), q, right, 0)
        arrive(plane(1, 1), q)
        push(plane(1, 1), q, left, 1)
        add(plane(1, 3), q)
        add(plane(1, 1), q)
    outs = []

    def store(q):
        rows = pl.ds(pl.multiple_of(q * (ROW_TILES * LANE), LANE), ROW_TILES * LANE)
        cp = pltpu.make_async_copy(acc.at[rows], out.at[rows], out_sem.at[len(outs)])
        cp.start()
        outs.append(cp)

    for dx in range(NX):
        arrive(plane(1, dx), q0)
        add(plane(1, dx), q0)
    store(q0)
    for dh in rest:
        q = chunk[dh]
        arrive(plane(1, 2), q, 0)
        arrive(plane(1, 2), q, 1)
        add(plane(1, 2), q)
        store(q)
    for cp in sends1 + sends2 + sends3:
        cp.wait_send()
    for cp in outs:
        cp.wait()


N_SENDS3 = 2 + 2 + 4 + 3 * (3 + 2 + 2 + 2)


def on_device(update, resident, placement, counts):
    _, rows, cols = resident.shape
    bf16 = jnp.bfloat16
    result = pl.pallas_call(
        kernel,
        out_shape=jax.ShapeDtypeStruct((rows, cols), bf16),
        in_specs=[
            pl.BlockSpec(memory_space=pl.ANY),
            pl.BlockSpec(memory_space=pl.ANY),
            pl.BlockSpec(memory_space=pltpu.SMEM),
            pl.BlockSpec(memory_space=pltpu.SMEM),
        ],
        out_specs=pl.BlockSpec(memory_space=pl.ANY),
        scratch_shapes=[
            pltpu.VMEM((EXP * TPD, LANE, LANE), jnp.float32),
            pltpu.VMEM((rows, cols), bf16),
            pltpu.VMEM((rows, cols), bf16),
            pltpu.VMEM((NL, EXP * TPD, SLAB, LANE), bf16),
            pltpu.VMEM((NL, EXP * TPD, SLAB, LANE), bf16),
            pltpu.VMEM((NE - 1, TPD, SLAB, LANE), bf16),
            pltpu.VMEM((NL, NH, BLK, SLAB, LANE), bf16),
            pltpu.SMEM((NE,), jnp.int32),
            pltpu.SemaphoreType.DMA,
            pltpu.SemaphoreType.DMA,
            pltpu.SemaphoreType.DMA((NH,)),
            pltpu.SemaphoreType.DMA((NL - 1,)),
            pltpu.SemaphoreType.DMA((NL,)),
            pltpu.SemaphoreType.DMA((NE - 1,)),
            pltpu.SemaphoreType.DMA((NE,)),
            pltpu.SemaphoreType.DMA((N_SENDS3,)),
            pltpu.SemaphoreType.DMA((NL, NH, 2)),
        ],
        compiler_params=pltpu.CompilerParams(collective_id=0, has_side_effects=True, vmem_limit_bytes=40 << 20),
        name="refresh",
    )(update.reshape(EXP * TPD, LANE, LANE), resident.reshape(rows, cols), placement, counts)
    return result[None]


def solution(mesh):
    placed = (P("learn", "expert", None, None), P("expert", None, None), P(), P())
    return jax.shard_map(
        on_device, mesh=mesh, in_specs=placed, out_specs=P("expert", None, None), check_vma=False
    )
```

time: 265 us -> 81 us (0.31)
  waiting for transfers between devices: 151 us -> 0 us
  Pallas kernels: 0 us -> 73.4 us
  local copies, waits for them, and re-layouts: 32.8 us -> 7.47 us
  starting transfers between devices: 24.3 us -> 0 us
  other arithmetic: 23.9 us -> 0 us
  blocking collectives: 16.4 us -> 0 us
  between operations: 15.4 us -> 0.01 us
    all_to_all x2 -> x0, waiting for transfers between devices: 115 us -> none  [the longest x1 115 us: on_device(): lax.all_to_all(ordered_codes, 'expert', split_axis=0, concat_axis=1, tile...]
    pallas_call x0 -> x1, Pallas kernels: none -> 73.4 us  [on_device(): pl.pallas_call(kernel, out_shape=jax.ShapeDtypeStruct((rows, cols), bf16)...]
    all_gather x1 -> x0, waiting for transfers between devices: 36.2 us -> none  [on_device(): lax.all_gather(code_tiles, 'learn', axis=0, tiled=True)]
    all_to_all x2 -> x0, starting transfers between devices: 24.2 us -> none  [the longest x1 14.7 us: on_device(): lax.all_to_all(ordered_scales, 'expert', split_axis=0, concat_axis=1, til...]
    all_gather x1 -> x0, blocking collectives: 16.4 us -> none  [on_device(): lax.all_gather(block_scale, 'learn', axis=0, tiled=True)]
    transpose x1 -> x0, local copies, waits for them, and re-layouts: 12.7 us -> none  [apply_delta(): window = window.transpose(0, 2, 1, 3).reshape(row_count, col_count)]
    convert_element_type x3 -> x0, other arithmetic: 12.2 us -> none  [the longest x1 9.82 us: apply_delta(): return (resident[0].astype(jnp.float32) + window).astype(jnp.bfloat16)[None]]
    reshape x1 -> x0, local copies, waits for them, and re-layouts: 11.4 us -> none  [apply_delta(): window = window.transpose(0, 2, 1, 3).reshape(row_count, col_count)]
  transfers between devices with their start and end apart: 3 -> 0, of which waited for: 2 -> 0; matrix products, arithmetic and copies ran while one was open for 6% -> 0% of each run, Pallas kernels for 0% -> 0%
where the time goes in v1:
time: 81 us; the launch traced here: 80.9 us
  Pallas kernels  73.4 us (91%)
  local copies, waits for them, and re-layouts  7.47 us (9%)
    pallas_call x1, Pallas kernels, on_device(): pl.pallas_call(kernel, out_shape=jax.ShapeDtypeStruct((rows, cols), bf16)...  73.4 us
    unnamed x9, local copies, waits for them, and re-layouts  7.47 us

profile of v1, /device:TPU:1, one launch (start us, length us, event | category | flops | bytes accessed | tf_op | source)
XLA Modules:
  0.0 80.9 jit_solution(290735141632617598)
XLA Ops:
  0.0 0.0 copy-start
  0.0 2.5 %copy-done = bf16[1,2560,1024]{2,1,0:T(8,128)(2,1)S(1)} copy-done((bf16[1,2560,1024]{2,1,0:T(8,128)(2,1)S(1)}, bf16[1,2560,1024]{2,1,0:T(8,128)(2,1)}, u32[]{:S(2)}) %copy-start) | copy-done | bytes 5242904
  2.5 0.0 copy-start.1
  2.5 1.3 %copy-done.1 = f32[4,5,128,128]{3,2,1,0:T(8,128)S(1)} copy-done((f32[4,5,128,128]{3,2,1,0:T(8,128)S(1)}, f32[4,5,128,128]{3,2,1,0:T(8,128)}, u32[]{:S(2)}) %copy-start.1) | copy-done | bytes 1310744
  3.8 0.0 copy-start.2
  3.8 0.7 copy-done.2
  4.5 0.0 copy-start.3
  4.5 0.7 copy-done.3
  5.1 73.4 %refresh.1 = bf16[2560,1024]{1,0:T(8,128)(2,1)S(1)} custom-call(f32[20,128,128]{2,1,0:T(8,128)S(1)} %bitcast.5, bf16[2560,1024]{1,0:T(8,128)(2,1)S(1)} %bitcast.4, s32[32]{0:T(128)S(1)} %copy-done.2, s32[32]{0:T(128)S(1)} %copy-done.3), custom_call_target="tpu_custom_call" | custom-call | tf_op jit(solution)/shard_map/refresh/pallas_call | solution.py:230
  78.5 2.4 %copy.6 = bf16[1,2560,1024]{2,1,0:T(8,128)(2,1)} copy(bf16[1,2560,1024]{2,1,0:T(8,128)(2,1)S(1)} %bitcast.3) | data formatting | bytes 10485760
Async XLA Ops:
  0.0 2.5 %copy-start = (bf16[1,2560,1024]{2,1,0:T(8,128)(2,1)S(1)}, bf16[1,2560,1024]{2,1,0:T(8,128)(2,1)}, u32[]{:S(2)}) copy-start(bf16[1,2560,1024]{2,1,0:T(8,128)(2,1)} %param.5) | copy-start | bytes 15728644
  2.5 1.3 %copy-start.1 = (f32[4,5,128,128]{3,2,1,0:T(8,128)S(1)}, f32[4,5,128,128]{3,2,1,0:T(8,128)}, u32[]{:S(2)}) copy-start(f32[4,5,128,128]{3,2,1,0:T(8,128)} %param.4) | copy-start | bytes 3932164
  3.8 0.7 copy-start.2
  4.5 0.7 copy-start.3

commit v2 on v0

v2 whole, which is shorter than its diff:
```python
import jax
import jax.numpy as jnp
from jax import lax
from jax.experimental import pallas as pl
from jax.experimental.pallas import tpu as pltpu
from jax.sharding import PartitionSpec as P

MESH = pl.DeviceIdType.MESH
NX, NZ, NH, NY, NC = 4, 2, 4, 4, 2
NL, NE = 8, 32
EXP, PER, TPD = 4, 8, 5
SLAB, LANE = 16, 128
BLK = 40
SIDE = NY * NC
VMEM_LIMIT = 48 << 20
ROW_TILES = 5


def kernel(update, resident, placement_in, counts_in, out,
           upd, res, s1, r1, s2, gat, placement, counts, owner,
           in_sem, s1_send, s1_recv, s2_send, s2_recv, g_send, g_recv):
    l = lax.axis_index("learn")
    e = lax.axis_index("expert")
    zl, x = l // NX, l % NX
    zh, y, c = e // (NY * NC), (e // NC) % NY, e % NC
    right = (zl * NX + (x + 1) % NX, e)
    left = (zl * NX + (x + 3) % NX, e)
    across = ((1 - zl) * NX + x, e)

    ins = []
    for n, (src, dst) in enumerate(((counts_in, counts), (update, upd), (placement_in, placement), (resident, res))):
        cp = pltpu.make_async_copy(src, dst, in_sem.at[n])
        cp.start()
        ins.append(cp)
    counts_ready, upd_ready, placement_ready, res_ready = ins

    learn_peers = [(((zl + dz) % NZ) * NX + (x + dx) % NX) for dz in range(NZ) for dx in range(NX) if (dz, dx) != (0, 0)]

    def slot(dh, n):
        return ((zh + dh) % NH) * SIDE + (((y + n // NC) % NY) * NC + (c + n) % NC)

    def zl_at(dh):
        return {0: zl, 1: 0, 3: 1, 2: 1 - zl}[dh]

    def sources(dh):
        back = (4 - dh) % NH
        if dh == 0:
            return [(zl, slot(0, n)) for n in range(1, SIDE)]
        if dh == 2:
            return [(1 - zl, slot(2, n)) for n in range(SIDE)]
        at = (zh + 3 + 2 * zl) % NH
        source_zl = zl if dh == 1 else 1 - zl
        return [(source_zl, at * SIDE + slot(0, n) % SIDE) for n in range(SIDE)]

    targets = {dh: [(zl_at(dh) * NX + x, slot(dh, n)) for n in range(1 if dh == 0 else 0, SIDE)] for dh in (0, 1, 3, 2)}

    barrier = pltpu.get_barrier_semaphore()
    for peer in learn_peers:
        pl.semaphore_signal(barrier, inc=1, device_id=(peer, e), device_id_type=MESH)
    for dh in (0, 1, 3, 2):
        for source_zl, k in sources(dh):
            pl.semaphore_signal(barrier, inc=1, device_id=(source_zl * NX + x, k), device_id_type=MESH)

    counts_ready.wait()
    upd_ready.wait()

    def encode(t, carry):
        u = upd[t]
        largest = jnp.max(jnp.abs(u), axis=(0, 1), keepdims=True)
        scale = ((largest + 1e-06) / 448.0).astype(jnp.bfloat16).astype(jnp.float32)
        code = (u * (1.0 / scale)).astype(jnp.bfloat16).astype(jnp.float32)
        changed = jnp.where(e * TPD + t % TPD < counts[l * EXP + t // TPD], 1.0, 0.0).astype(jnp.float32)
        s1[:, t] = (code * (scale * changed)).astype(jnp.bfloat16).reshape(NL, SLAB, LANE)
        return carry

    lax.fori_loop(0, EXP * TPD, encode, 0, unroll=5)
    pl.semaphore_wait(barrier, NL - 1 + NE - 1)

    sends = []
    for n, peer in enumerate(learn_peers):
        cp = pltpu.make_async_remote_copy(
            src_ref=s1.at[peer], dst_ref=r1.at[l], send_sem=s1_send.at[n], recv_sem=s1_recv.at[l],
            device_id=(peer, e), device_id_type=MESH)
        cp.start()
        sends.append(cp)
    r1[l] = s1[l]
    placement_ready.wait()

    def owner_of(k, carry):
        def step(n, best):
            return jnp.maximum(best, jnp.where(placement[n] == k, n, 0))
        owner[k] = lax.fori_loop(0, NE, step, 0, unroll=True)
        return carry

    lax.fori_loop(0, NE, owner_of, 0)
    res_ready.wait()
    for peer in learn_peers:
        pltpu.make_async_remote_copy(
            src_ref=r1.at[peer], dst_ref=r1.at[peer], send_sem=s1_send.at[0], recv_sem=s1_recv.at[peer],
            device_id=(peer, e), device_id_type=MESH).wait_recv()

    mine = pl.ds((y * NC + c) * TPD, TPD)

    def picked(k):
        o = owner[k]
        return r1[o // EXP, pl.ds((o % EXP) * TPD, TPD)]

    sent = [0]

    def send_to(dh):
        for peer, k in targets[dh]:
            n = sent[0]
            sent[0] += 1
            s2[n] = picked(k)
            cp = pltpu.make_async_remote_copy(
                src_ref=s2.at[n], dst_ref=gat.at[l, zh, mine],
                send_sem=s2_send.at[n], recv_sem=s2_recv.at[zl, e],
                device_id=(peer, k), device_id_type=MESH)
            cp.start()
            sends.append(cp)

    def receive(dh):
        for source_zl, k in sources(dh):
            ref = gat.at[source_zl * NX + x, k // SIDE, pl.ds((k % SIDE) * TPD, TPD)]
            pltpu.make_async_remote_copy(
                src_ref=ref, dst_ref=ref, send_sem=s2_send.at[0], recv_sem=s2_recv.at[source_zl, k],
                device_id=across, device_id_type=MESH).wait_recv()

    pushed = [0]

    def part(src, q, half):
        if half is None:
            return gat.at[src, q]
        return gat.at[src, q, pl.ds(half * (BLK // 2), BLK // 2)]

    def push(src, q, to, half=None):
        ref = part(src, q, half)
        cp = pltpu.make_async_remote_copy(
            src_ref=ref, dst_ref=ref, send_sem=g_send.at[pushed[0]], recv_sem=g_recv.at[src, q, 0 if half is None else half],
            device_id=to, device_id_type=MESH)
        cp.start()
        pushed[0] += 1
        sends.append(cp)

    def arrive(src, q, half=None):
        ref = part(src, q, half)
        pltpu.make_async_remote_copy(
            src_ref=ref, dst_ref=ref, send_sem=g_send.at[0], recv_sem=g_recv.at[src, q, 0 if half is None else half],
            device_id=across, device_id_type=MESH).wait_recv()

    def add(src, q):
        def row(a, carry):
            at = pl.multiple_of((q * ROW_TILES + a) * LANE + src * SLAB, SLAB)
            for b in range(8):
                cols = pl.ds(b * LANE, LANE)
                out[pl.ds(at, SLAB), cols] = (
                    res[pl.ds(at, SLAB), cols].astype(jnp.float32) + gat[src, q, a * 8 + b].astype(jnp.float32)
                ).astype(jnp.bfloat16)
            return carry
        lax.fori_loop(0, ROW_TILES, row, 0)

    q1 = (zh + 3 + 2 * zl) % NH
    v1 = (zh + 1 + 2 * zl) % NH
    q2 = (zh + 2) % NH
    other = 1 - zl
    U = [(zl, zh), (zl, q1), (other, q1), (other, q2)]
    V = [(other, zh), (other, v1), (zl, v1), (zl, q2)]

    def at(unit, dx):
        return (unit[0] * NX + (x + dx) % NX, unit[1])

    def spread(unit):
        push(*at(unit, 0), right)
        push(*at(unit, 0), left)

    def relay(unit):
        arrive(*at(unit, 3))
        push(*at(unit, 3), right, 0)
        arrive(*at(unit, 1))
        push(*at(unit, 1), left, 1)

    def added(unit, *steps):
        for dx in steps:
            add(*at(unit, dx))

    def finish(unit):
        arrive(*at(unit, 2), 0)
        arrive(*at(unit, 2), 1)
        add(*at(unit, 2))

    send_to(0)
    gat[l, zh, mine] = picked(e)
    send_to(1)
    send_to(3)
    receive(0)
    spread(U[0])
    send_to(2)
    added(U[0], 0)
    relay(U[0])
    added(U[0], 3, 1)
    for n, dh in ((2, 3), (1, 1)):
        receive(dh)
        push(*at(U[n], 0), across)
        spread(U[n])
        added(U[n], 0)
    finish(U[0])
    for n in (2, 1):
        relay(U[n])
        added(U[n], 3, 1)
    receive(2)
    push(*at(U[3], 0), across)
    spread(U[3])
    added(U[3], 0)
    for dx in range(NX):
        push(*at(U[0], dx), across)
    for n in (2, 1):
        arrive(*at(V[n], 0))
        spread(V[n])
        added(V[n], 0)
    relay(U[3])
    added(U[3], 3, 1)
    finish(U[2])
    finish(U[1])
    arrive(*at(V[3], 0))
    spread(V[3])
    added(V[3], 0)
    for n in (2, 1):
        relay(V[n])
        added(V[n], 3, 1)
    finish(U[3])
    relay(V[3])
    added(V[3], 3, 1)
    for dx in range(NX):
        arrive(*at(V[0], dx))
        added(V[0], dx)
    for n in (2, 1, 3):
        finish(V[n])
    for cp in sends:
        cp.wait_send()


N_PUSH = 2 + 2 + 4 + 3 * (3 + 2 + 2 + 2)


def on_device(update, resident, placement, counts):
    _, rows, cols = resident.shape
    bf16 = jnp.bfloat16
    dma = pltpu.SemaphoreType.DMA
    result = pl.pallas_call(
        kernel,
        out_shape=pltpu.VMEM((rows, cols), bf16),
        in_specs=[pl.BlockSpec(memory_space=pltpu.HBM)] * 4,
        out_specs=pl.BlockSpec(memory_space=pltpu.VMEM),
        scratch_shapes=[
            pltpu.VMEM((EXP * TPD, LANE, LANE), jnp.float32),
            pltpu.VMEM((rows, cols), bf16),
            pltpu.VMEM((NL, EXP * TPD, SLAB, LANE), bf16),
            pltpu.VMEM((NL, EXP * TPD, SLAB, LANE), bf16),
            pltpu.VMEM((NE - 1, TPD, SLAB, LANE), bf16),
            pltpu.VMEM((NL, NH, BLK, SLAB, LANE), bf16),
            pltpu.SMEM((NE,), jnp.int32),
            pltpu.SMEM((NE,), jnp.int32),
            pltpu.SMEM((NE,), jnp.int32),
            dma((4,)),
            dma((NL - 1,)),
            dma((NL,)),
            dma((NE - 1,)),
            dma((NZ, NE)),
            dma((N_PUSH,)),
            dma((NL, NH, 2)),
        ],
        compiler_params=pltpu.CompilerParams(collective_id=0, has_side_effects=True, vmem_limit_bytes=VMEM_LIMIT),
        name="refresh",
    )(*(pltpu.with_memory_space_constraint(a, pltpu.HBM) for a in (update.reshape(EXP * TPD, LANE, LANE), resident.reshape(rows, cols), placement, counts)))
    return result[None]


def solution(mesh):
    placed = (P("learn", "expert", None, None), P("expert", None, None), P(), P())
    return jax.shard_map(
        on_device, mesh=mesh, in_specs=placed, out_specs=P("expert", None, None), check_vma=False
    )
```

time: 265 us -> 71.5 us (0.27)
  waiting for transfers between devices: 151 us -> 0 us
  Pallas kernels: 0 us -> 68.6 us
  local copies, waits for them, and re-layouts: 32.8 us -> 2.36 us
  starting transfers between devices: 24.3 us -> 0 us
  other arithmetic: 23.9 us -> 0 us
  blocking collectives: 16.4 us -> 0 us
  between operations: 15.4 us -> 0.01 us
    all_to_all x2 -> x0, waiting for transfers between devices: 115 us -> none  [the longest x1 115 us: on_device(): lax.all_to_all(ordered_codes, 'expert', split_axis=0, concat_axis=1, tile...]
    pallas_call x0 -> x1, Pallas kernels: none -> 68.6 us  [on_device(): pl.pallas_call(kernel, out_shape=pltpu.VMEM((rows, cols), bf16), in_specs...]
    all_gather x1 -> x0, waiting for transfers between devices: 36.2 us -> none  [on_device(): lax.all_gather(code_tiles, 'learn', axis=0, tiled=True)]
    all_to_all x2 -> x0, starting transfers between devices: 24.2 us -> none  [the longest x1 14.7 us: on_device(): lax.all_to_all(ordered_scales, 'expert', split_axis=0, concat_axis=1, til...]
    all_gather x1 -> x0, blocking collectives: 16.4 us -> none  [on_device(): lax.all_gather(block_scale, 'learn', axis=0, tiled=True)]
    transpose x1 -> x0, local copies, waits for them, and re-layouts: 12.7 us -> none  [apply_delta(): window = window.transpose(0, 2, 1, 3).reshape(row_count, col_count)]
    convert_element_type x3 -> x0, other arithmetic: 12.2 us -> none  [the longest x1 9.82 us: apply_delta(): return (resident[0].astype(jnp.float32) + window).astype(jnp.bfloat16)[None]]
    reshape x1 -> x0, local copies, waits for them, and re-layouts: 11.4 us -> none  [apply_delta(): window = window.transpose(0, 2, 1, 3).reshape(row_count, col_count)]
  transfers between devices with their start and end apart: 3 -> 0, of which waited for: 2 -> 0; matrix products, arithmetic and copies ran while one was open for 6% -> 0% of each run, Pallas kernels for 0% -> 0%
where the time goes in v2:
time: 71.5 us; the launch traced here: 71 us
  Pallas kernels  68.6 us (96%)
  local copies, waits for them, and re-layouts  2.36 us (3%)
    pallas_call x1, Pallas kernels, on_device(): pl.pallas_call(kernel, out_shape=pltpu.VMEM((rows, cols), bf16), in_specs...  68.6 us
    unnamed x1, local copies, waits for them, and re-layouts  2.36 us

profile of v2, /device:TPU:1, one launch (start us, length us, event | category | flops | bytes accessed | tf_op | source)
XLA Modules:
  0.0 71.0 jit_solution(5160600192355071040)
XLA Ops:
  0.0 68.6 %refresh.1 = bf16[2560,1024]{1,0:T(8,128)(2,1)S(1)} custom-call(f32[20,128,128]{2,1,0:T(8,128)} %bitcast.5, bf16[2560,1024]{1,0:T(8,128)(2,1)} %bitcast.4, s32[32]{0:T(128)} %placement_in.1, s32[32]{0:T(128)} %counts_in.1), custom_call_target="tpu_custom_call" | custom-call | tf_op jit(solution)/shard_map/refresh/pallas_call | solution.py:249
  68.6 2.4 %copy.6 = bf16[1,2560,1024]{2,1,0:T(8,128)(2,1)} copy(bf16[1,2560,1024]{2,1,0:T(8,128)(2,1)S(1)} %bitcast.3) | data formatting | bytes 10485760

commit v3 on v2

v3 whole, which is shorter than its diff:
```python
import jax
import jax.numpy as jnp
from jax import lax
from jax.experimental import pallas as pl
from jax.experimental.pallas import tpu as pltpu
from jax.sharding import PartitionSpec as P

MESH = pl.DeviceIdType.MESH
NX, NZ, NH, NY, NC = 4, 2, 4, 4, 2
NL, NE = 8, 32
EXP, PER, TPD = 4, 8, 5
SLAB, LANE = 16, 128
SIDE = NY * NC
VMEM_LIMIT = 48 << 20
PARTS = ((0, 3), (3, 2))
WHOLE = (0, TPD)
ROW_TILES = 5


def kernel(update, resident, placement_in, counts_in, out,
           upd, res, s1a, s1b, r1a, r1b, s2, gat, placement, counts, owner,
           in_sem, s1_send, s1_recv, s2_send, s2_recv, g_send, g_recv):
    l = lax.axis_index("learn")
    e = lax.axis_index("expert")
    zl, x = l // NX, l % NX
    zh, y, c = e // (NY * NC), (e // NC) % NY, e % NC
    right = (zl * NX + (x + 1) % NX, e)
    left = (zl * NX + (x + 3) % NX, e)
    across = ((1 - zl) * NX + x, e)

    ins = []
    for n, (src, dst) in enumerate(((counts_in, counts), (update, upd), (placement_in, placement), (resident, res))):
        cp = pltpu.make_async_copy(src, dst, in_sem.at[n])
        cp.start()
        ins.append(cp)
    counts_ready, upd_ready, placement_ready, res_ready = ins

    learn_peers = [(((zl + dz) % NZ) * NX + (x + dx) % NX) for dz in range(NZ) for dx in range(NX) if (dz, dx) != (0, 0)]

    def slot(dh, n):
        return ((zh + dh) % NH) * SIDE + (((y + n // NC) % NY) * NC + (c + n) % NC)

    def zl_at(dh):
        return {0: zl, 1: 0, 3: 1, 2: 1 - zl}[dh]

    def sources(dh):
        back = (4 - dh) % NH
        if dh == 0:
            return [(zl, slot(0, n)) for n in range(1, SIDE)]
        if dh == 2:
            return [(1 - zl, slot(2, n)) for n in range(SIDE)]
        at = (zh + 3 + 2 * zl) % NH
        source_zl = zl if dh == 1 else 1 - zl
        return [(source_zl, at * SIDE + slot(0, n) % SIDE) for n in range(SIDE)]

    targets = {dh: [(zl_at(dh) * NX + x, slot(dh, n)) for n in range(1 if dh == 0 else 0, SIDE)] for dh in (0, 1, 3, 2)}

    barrier = pltpu.get_barrier_semaphore()
    for peer in learn_peers:
        pl.semaphore_signal(barrier, inc=1, device_id=(peer, e), device_id_type=MESH)
    for dh in (0, 1, 3, 2):
        for source_zl, k in sources(dh):
            pl.semaphore_signal(barrier, inc=1, device_id=(source_zl * NX + x, k), device_id_type=MESH)

    s1, r1 = (s1a, s1b), (r1a, r1b)

    counts_ready.wait()
    upd_ready.wait()

    def encode_part(p):
        first, size = PARTS[p]

        def encode(n, carry):
            i, m = n // size, n % size
            j = first + m
            u = upd[i, j]
            largest = jnp.max(jnp.abs(u), axis=(0, 1), keepdims=True)
            scale = ((largest + 1e-06) / 448.0).astype(jnp.bfloat16).astype(jnp.float32)
            code = (u * (1.0 / scale)).astype(jnp.bfloat16).astype(jnp.float32)
            changed = jnp.where(e * TPD + j < counts[l * EXP + i], 1.0, 0.0).astype(jnp.float32)
            s1[p][:, i, m] = (code * (scale * changed)).astype(jnp.bfloat16).reshape(NL, SLAB, LANE)
            return carry

        lax.fori_loop(0, EXP * size, encode, 0, unroll=4)

    def wait_for(ref, sem):
        pltpu.make_async_copy(ref, ref, sem).wait()

    def exchange(p):
        for peer in learn_peers:
            cp = pltpu.make_async_remote_copy(
                src_ref=s1[p].at[peer], dst_ref=r1[p].at[l],
                send_sem=s1_send.at[p], recv_sem=s1_recv.at[p],
                device_id=(peer, e), device_id_type=MESH)
            cp.start()

    def exchanged(p):
        wait_for(r1[p].at[pl.ds(0, NL - 1)], s1_recv.at[p])

    encode_part(0)
    pl.semaphore_wait(barrier, NL - 1 + NE - 1)
    exchange(0)
    encode_part(1)
    exchange(1)
    for p in range(2):
        r1[p][l] = s1[p][l]
    placement_ready.wait()

    def owner_of(k, carry):
        def step(n, best):
            return jnp.maximum(best, jnp.where(placement[n] == k, n, 0))
        owner[k] = lax.fori_loop(0, NE, step, 0, unroll=True)
        return carry

    lax.fori_loop(0, NE, owner_of, 0)
    res_ready.wait()

    me = y * NC + c

    def pick(ref, k, span):
        o = owner[k]
        for p, part in enumerate(PARTS):
            if span in (part, WHOLE):
                ref[pl.ds(*part)] = r1[p][o // EXP, o % EXP]

    def send_to(dh, span, p):
        group = {0: 0, 1: jnp.where(zl == 0, 1, 2), 3: jnp.where(zl == 1, 1, 2), 2: 3}[dh]
        for m, (peer, k) in enumerate(targets[dh]):
            n = ORDER[dh] + m
            pick(s2.at[n], k, span)
            pltpu.make_async_remote_copy(
                src_ref=s2.at[n, pl.ds(*span)], dst_ref=gat.at[l, zh, me, pl.ds(*span)],
                send_sem=s2_send, recv_sem=s2_recv.at[p, group],
                device_id=(peer, k), device_id_type=MESH).start()

    def own_part(span):
        pick(gat.at[l, zh, me], e, span)

    def receive(group, span, p):
        first = 1 if group == 0 else 0
        wait_for(gat.at[l, zh, pl.ds(first, SIDE - first), pl.ds(*span)], s2_recv.at[p, group])

    def piece(src, q, span, half):
        if half is None:
            return gat.at[src, q, :, pl.ds(*span)]
        return gat.at[src, q, pl.ds(half * (SIDE // 2), SIDE // 2), pl.ds(*span)]

    def slot_of(span, half):
        return (1 if span == PARTS[1] else 0) * 2 + (half or 0)

    def push(src, q, span, to, half=None):
        ref = piece(src, q, span, half)
        pltpu.make_async_remote_copy(
            src_ref=ref, dst_ref=ref, send_sem=g_send, recv_sem=g_recv.at[src, q, slot_of(span, half)],
            device_id=to, device_id_type=MESH).start()

    def arrive(src, q, span, half=None):
        wait_for(piece(src, q, span, half), g_recv.at[src, q, slot_of(span, half)])

    def add(src, q):
        def row(a, carry):
            at = pl.multiple_of((q * ROW_TILES + a) * LANE + src * SLAB, SLAB)
            for b in range(8):
                cols = pl.ds(b * LANE, LANE)
                t = a * 8 + b
                out[pl.ds(at, SLAB), cols] = (
                    res[pl.ds(at, SLAB), cols].astype(jnp.float32) + gat[src, q, t // TPD, t % TPD].astype(jnp.float32)
                ).astype(jnp.bfloat16)
            return carry
        lax.fori_loop(0, ROW_TILES, row, 0)

    q1 = (zh + 3 + 2 * zl) % NH
    v1 = (zh + 1 + 2 * zl) % NH
    q2 = (zh + 2) % NH
    other = 1 - zl
    U = [(zl, zh), (zl, q1), (other, q1), (other, q2)]
    V = [(other, zh), (other, v1), (zl, v1), (zl, q2)]
    A, B = PARTS

    def at(unit, dx):
        return (unit[0] * NX + (x + dx) % NX, unit[1])

    def spread(unit, span):
        push(*at(unit, 0), span, right)
        push(*at(unit, 0), span, left)

    def relay(unit, *spans):
        for dx, to, half in ((3, right, 0), (1, left, 1)):
            for span in spans:
                arrive(*at(unit, dx), span)
            push(*at(unit, dx), WHOLE, to, half)

    def added(unit, *steps):
        for dx in steps:
            add(*at(unit, dx))

    def finish(unit):
        arrive(*at(unit, 2), WHOLE, 0)
        arrive(*at(unit, 2), WHOLE, 1)
        add(*at(unit, 2))

    def cross(unit):
        push(*at(unit, 0), WHOLE, across)

    def crossed(unit):
        arrive(*at(unit, 0), WHOLE)
        spread(unit, WHOLE)

    exchanged(0)
    send_to(0, A, 0)
    own_part(A)
    send_to(1, A, 0)
    send_to(3, A, 0)
    receive(0, A, 0)
    spread(U[0], A)
    exchanged(1)
    send_to(0, B, 1)
    own_part(B)
    send_to(1, B, 1)
    send_to(3, B, 1)
    receive(0, B, 1)
    spread(U[0], B)
    send_to(2, WHOLE, 0)
    added(U[0], 0)
    for n in (2, 1):
        receive(n, A, 0)
        spread(U[n], A)
    relay(U[0], A, B)
    added(U[0], 3, 1)
    for n in (2, 1):
        receive(n, B, 1)
        cross(U[n])
        spread(U[n], B)
        added(U[n], 0)
    finish(U[0])
    for n in (2, 1):
        relay(U[n], A, B)
        added(U[n], 3, 1)
    for n in (2, 1):
        crossed(V[n])
        added(V[n], 0)
    receive(3, WHOLE, 0)
    cross(U[3])
    spread(U[3], WHOLE)
    added(U[3], 0)
    for dx in range(NX):
        push(*at(U[0], dx), WHOLE, across)
    for n in (2, 1):
        finish(U[n])
        relay(V[n], WHOLE)
        added(V[n], 3, 1)
    relay(U[3], WHOLE)
    added(U[3], 3, 1)
    crossed(V[3])
    added(V[3], 0)
    for n in (2, 1):
        finish(V[n])
    finish(U[3])
    relay(V[3], WHOLE)
    added(V[3], 3, 1)
    for dx in range(NX):
        arrive(*at(V[0], dx), WHOLE)
        added(V[0], dx)
    for p in range(2):
        wait_for(s1[p].at[pl.ds(0, NL - 1)], s1_send.at[p])
    wait_for(s2, s2_send)
    finish(V[3])
    wait_for(gat.at[pl.ds(0, NL - 1)], g_send)


ORDER = {0: 0, 1: SIDE - 1, 3: 2 * SIDE - 1, 2: 3 * SIDE - 1}


def on_device(update, resident, placement, counts):
    _, rows, cols = resident.shape
    bf16 = jnp.bfloat16
    dma = pltpu.SemaphoreType.DMA
    result = pl.pallas_call(
        kernel,
        out_shape=pltpu.VMEM((rows, cols), bf16),
        in_specs=[pl.BlockSpec(memory_space=pltpu.HBM)] * 4,
        out_specs=pl.BlockSpec(memory_space=pltpu.VMEM),
        scratch_shapes=[
            pltpu.VMEM((EXP, TPD, LANE, LANE), jnp.float32),
            pltpu.VMEM((rows, cols), bf16),
            *[pltpu.VMEM((NL, EXP, size, SLAB, LANE), bf16) for _ in range(2) for _, size in PARTS],
            pltpu.VMEM((NE - 1, TPD, SLAB, LANE), bf16),
            pltpu.VMEM((NL, NH, SIDE, TPD, SLAB, LANE), bf16),
            pltpu.SMEM((NE,), jnp.int32),
            pltpu.SMEM((NE,), jnp.int32),
            pltpu.SMEM((NE,), jnp.int32),
            dma((4,)),
            dma((2,)),
            dma((2,)),
            dma,
            dma((2, 4)),
            dma,
            dma((NL, NH, 4)),
        ],
        compiler_params=pltpu.CompilerParams(collective_id=0, has_side_effects=True, vmem_limit_bytes=VMEM_LIMIT),
        name="refresh",
    )(*(pltpu.with_memory_space_constraint(a, pltpu.HBM) for a in (update, resident.reshape(rows, cols), placement, counts)))
    return result[None]


def solution(mesh):
    placed = (P("learn", "expert", None, None), P("expert", None, None), P(), P())
    return jax.shard_map(
        on_device, mesh=mesh, in_specs=placed, out_specs=P("expert", None, None), check_vma=False
    )
```

time: 71.5 us -> 70.2 us (0.982)
  Pallas kernels: 68.6 us -> 66.7 us
    pallas_call x1, Pallas kernels: 68.6 us -> 66.7 us  [on_device(): pl.pallas_call(kernel, out_shape=pltpu.VMEM((rows, cols), bf16), in_specs...]
where the time goes in v3:
time: 70.2 us; the launch traced here: 69.1 us
  Pallas kernels  66.7 us (95%)
  local copies, waits for them, and re-layouts  2.36 us (3%)
    pallas_call x1, Pallas kernels, on_device(): pl.pallas_call(kernel, out_shape=pltpu.VMEM((rows, cols), bf16), in_specs...  66.7 us
    unnamed x1, local copies, waits for them, and re-layouts  2.36 us

profile of v3, /device:TPU:1, one launch (start us, length us, event | category | flops | bytes accessed | tf_op | source)
XLA Modules:
  0.0 69.1 jit_solution(8155468189154229091)
XLA Ops:
  0.0 66.7 %refresh.1 = bf16[2560,1024]{1,0:T(8,128)(2,1)S(1)} custom-call(f32[4,5,128,128]{3,2,1,0:T(8,128)} %update.1, bf16[2560,1024]{1,0:T(8,128)(2,1)} %bitcast.3, s32[32]{0:T(128)} %placement_in.1, s32[32]{0:T(128)} %counts_in.1), custom_call_target="tpu_custom_call" | custom-call | tf_op jit(solution)/shard_map/refresh/pallas_call | solution.py:278
  66.7 2.4 %copy.6 = bf16[1,2560,1024]{2,1,0:T(8,128)(2,1)} copy(bf16[1,2560,1024]{2,1,0:T(8,128)(2,1)S(1)} %bitcast.2) | data formatting | bytes 10485760

commit v4 on v3

--- a/solution.py
+++ b/solution.py
@@ -12,7 +12,7 @@
 SLAB, LANE = 16, 128
 SIDE = NY * NC
 VMEM_LIMIT = 48 << 20
-PARTS = ((0, 3), (3, 2))
+PARTS = ((0, 2), (2, 3))
 WHOLE = (0, TPD)
 ROW_TILES = 5
 
@@ -184,57 +184,66 @@
         push(*at(unit, 0), span, right)
         push(*at(unit, 0), span, left)
 
-    def relay(unit, *spans):
+    def relay(unit, span):
         for dx, to, half in ((3, right, 0), (1, left, 1)):
-            for span in spans:
-                arrive(*at(unit, dx), span)
-            push(*at(unit, dx), WHOLE, to, half)
+            arrive(*at(unit, dx), span)
+            push(*at(unit, dx), span, to, half)
 
     def added(unit, *steps):
         for dx in steps:
             add(*at(unit, dx))
 
-    def finish(unit):
-        arrive(*at(unit, 2), WHOLE, 0)
-        arrive(*at(unit, 2), WHOLE, 1)
+    def finish(unit, *spans):
+        for span in spans:
+            for half in range(2):
+                arrive(*at(unit, 2), span, half)
         add(*at(unit, 2))
 
-    def cross(unit):
-        push(*at(unit, 0), WHOLE, across)
+    def cross(unit, dx=0):
+        push(*at(unit, dx), WHOLE, across)
 
     def crossed(unit):
         arrive(*at(unit, 0), WHOLE)
         spread(unit, WHOLE)
 
+    def take(unit, *steps):
+        for dx in steps:
+            arrive(*at(unit, dx), WHOLE)
+            add(*at(unit, dx))
+
     exchanged(0)
     send_to(0, A, 0)
     own_part(A)
+    exchanged(1)
+    send_to(0, B, 1)
+    own_part(B)
     send_to(1, A, 0)
     send_to(3, A, 0)
     receive(0, A, 0)
     spread(U[0], A)
-    exchanged(1)
-    send_to(0, B, 1)
-    own_part(B)
     send_to(1, B, 1)
     send_to(3, B, 1)
     receive(0, B, 1)
     spread(U[0], B)
+    cross(U[0])
     send_to(2, WHOLE, 0)
     added(U[0], 0)
+    relay(U[0], A)
     for n in (2, 1):
         receive(n, A, 0)
         spread(U[n], A)
-    relay(U[0], A, B)
+    relay(U[0], B)
     added(U[0], 3, 1)
     for n in (2, 1):
         receive(n, B, 1)
         cross(U[n])
         spread(U[n], B)
         added(U[n], 0)
-    finish(U[0])
-    for n in (2, 1):
-        relay(U[n], A, B)
+    for n in (2, 1):
+        relay(U[n], A)
+    finish(U[0], A, B)
+    for n in (2, 1):
+        relay(U[n], B)
         added(U[n], 3, 1)
     for n in (2, 1):
         crossed(V[n])
@@ -243,28 +252,30 @@
     cross(U[3])
     spread(U[3], WHOLE)
     added(U[3], 0)
-    for dx in range(NX):
-        push(*at(U[0], dx), WHOLE, across)
-    for n in (2, 1):
-        finish(U[n])
-        relay(V[n], WHOLE)
-        added(V[n], 3, 1)
+    cross(U[0], 1)
+    finish(U[2], A, B)
+    cross(U[2], 2)
+    cross(U[0], 3)
+    cross(U[0], 2)
+    finish(U[1], A, B)
+    take(V[2], 3, 1)
+    relay(V[1], WHOLE)
+    added(V[1], 3, 1)
+    crossed(V[3])
+    added(V[3], 0)
     relay(U[3], WHOLE)
     added(U[3], 3, 1)
-    crossed(V[3])
-    added(V[3], 0)
-    for n in (2, 1):
-        finish(V[n])
-    finish(U[3])
+    take(V[2], 2)
+    finish(V[1], WHOLE)
+    take(V[0], 0, 1)
     relay(V[3], WHOLE)
     added(V[3], 3, 1)
-    for dx in range(NX):
-        arrive(*at(V[0], dx), WHOLE)
-        added(V[0], dx)
+    finish(U[3], WHOLE)
+    take(V[0], 3, 2)
+    finish(V[3], WHOLE)
     for p in range(2):
         wait_for(s1[p].at[pl.ds(0, NL - 1)], s1_send.at[p])
     wait_for(s2, s2_send)
-    finish(V[3])
     wait_for(gat.at[pl.ds(0, NL - 1)], g_send)
 
 

time: 70.2 us -> 65.4 us (0.932); the launches traced: 69.1 us -> 65.3 us
  Pallas kernels: 66.7 us -> 63 us
    pallas_call x1, Pallas kernels: 66.7 us -> 63 us  [on_device(): pl.pallas_call(kernel, out_shape=pltpu.VMEM((rows, cols), bf16), in_specs...]
where the time goes in v4:
time: 65.4 us; the launch traced here: 65.3 us
  Pallas kernels  63 us (96%)
  local copies, waits for them, and re-layouts  2.36 us (4%)
    pallas_call x1, Pallas kernels, on_device(): pl.pallas_call(kernel, out_shape=pltpu.VMEM((rows, cols), bf16), in_specs...  63 us
    unnamed x1, local copies, waits for them, and re-layouts  2.36 us

profile of v4, /device:TPU:1, one launch (start us, length us, event | category | flops | bytes accessed | tf_op | source)
XLA Modules:
  0.0 65.3 jit_solution(5119778566068418071)
XLA Ops:
  0.0 63.0 %refresh.1 = bf16[2560,1024]{1,0:T(8,128)(2,1)S(1)} custom-call(f32[4,5,128,128]{3,2,1,0:T(8,128)} %update.1, bf16[2560,1024]{1,0:T(8,128)(2,1)} %bitcast.3, s32[32]{0:T(128)} %placement_in.1, s32[32]{0:T(128)} %counts_in.1), custom_call_target="tpu_custom_call" | custom-call | tf_op jit(solution)/shard_map/refresh/pallas_call | solution.py:289
  63.0 2.4 %copy.6 = bf16[1,2560,1024]{2,1,0:T(8,128)(2,1)} copy(bf16[1,2560,1024]{2,1,0:T(8,128)(2,1)S(1)} %bitcast.2) | data formatting | bytes 10485760

commit v5 on v4

--- a/solution.py
+++ b/solution.py
@@ -18,7 +18,7 @@
 
 
 def kernel(update, resident, placement_in, counts_in, out,
-           upd, res, s1a, s1b, r1a, r1b, s2, gat, placement, counts, owner,
+           upd, res, s1a, s1b, r1a, r1b, s2, gat, placement, counts, inverse, owner,
            in_sem, s1_send, s1_recv, s2_send, s2_recv, g_send, g_recv):
     l = lax.axis_index("learn")
     e = lax.axis_index("expert")
@@ -40,27 +40,23 @@
     def slot(dh, n):
         return ((zh + dh) % NH) * SIDE + (((y + n // NC) % NY) * NC + (c + n) % NC)
 
-    def zl_at(dh):
-        return {0: zl, 1: 0, 3: 1, 2: 1 - zl}[dh]
-
-    def sources(dh):
-        back = (4 - dh) % NH
-        if dh == 0:
-            return [(zl, slot(0, n)) for n in range(1, SIDE)]
-        if dh == 2:
-            return [(1 - zl, slot(2, n)) for n in range(SIDE)]
-        at = (zh + 3 + 2 * zl) % NH
-        source_zl = zl if dh == 1 else 1 - zl
-        return [(source_zl, at * SIDE + slot(0, n) % SIDE) for n in range(SIDE)]
-
-    targets = {dh: [(zl_at(dh) * NX + x, slot(dh, n)) for n in range(1 if dh == 0 else 0, SIDE)] for dh in (0, 1, 3, 2)}
+    step = 2 * zl - 1
+    members = {0: (4, 5, 2, 3, 6, 7, 1)}
+    for group in (1, 2, 3):
+        members[group] = tuple(range(SIDE))
+
+    def peers(group, forward):
+        other = 1 - zl
+        dh, to_zl = {0: (0, zl), 1: (NH - step if forward else NH + step, zl),
+                     2: (NH + step, other), 3: (2, other)}[group]
+        return [(to_zl * NX + x, slot(dh, n)) for n in members[group]]
 
     barrier = pltpu.get_barrier_semaphore()
     for peer in learn_peers:
         pl.semaphore_signal(barrier, inc=1, device_id=(peer, e), device_id_type=MESH)
-    for dh in (0, 1, 3, 2):
-        for source_zl, k in sources(dh):
-            pl.semaphore_signal(barrier, inc=1, device_id=(source_zl * NX + x, k), device_id_type=MESH)
+    for group in (0, 2, 1, 3):
+        for peer, k in peers(group, False):
+            pl.semaphore_signal(barrier, inc=1, device_id=(peer, k), device_id_type=MESH)
 
     s1, r1 = (s1a, s1b), (r1a, r1b)
 
@@ -105,28 +101,26 @@
     for p in range(2):
         r1[p][l] = s1[p][l]
     placement_ready.wait()
-
-    def owner_of(k, carry):
-        def step(n, best):
-            return jnp.maximum(best, jnp.where(placement[n] == k, n, 0))
-        owner[k] = lax.fori_loop(0, NE, step, 0, unroll=True)
-        return carry
-
-    lax.fori_loop(0, NE, owner_of, 0)
+    ids = lax.broadcasted_iota(jnp.int32, (NE, NE), 1)
+    slots = lax.broadcasted_iota(jnp.int32, (NE, NE), 0)
+    held = jnp.where(placement[...] == slots, ids, 0)
+    inverse[...] = jnp.broadcast_to(jnp.max(held, axis=1, keepdims=True), (NE, LANE))
+    owner_in = pltpu.make_async_copy(inverse, owner, in_sem.at[4])
+    owner_in.start()
     res_ready.wait()
+    owner_in.wait()
 
     me = y * NC + c
 
     def pick(ref, k, span):
-        o = owner[k]
+        o = owner[k, 0]
         for p, part in enumerate(PARTS):
             if span in (part, WHOLE):
                 ref[pl.ds(*part)] = r1[p][o // EXP, o % EXP]
 
-    def send_to(dh, span, p):
-        group = {0: 0, 1: jnp.where(zl == 0, 1, 2), 3: jnp.where(zl == 1, 1, 2), 2: 3}[dh]
-        for m, (peer, k) in enumerate(targets[dh]):
-            n = ORDER[dh] + m
+    def send_to(group, span, p):
+        for m, (peer, k) in enumerate(peers(group, True)):
+            n = FIRST[group] + m
             pick(s2.at[n], k, span)
             pltpu.make_async_remote_copy(
                 src_ref=s2.at[n, pl.ds(*span)], dst_ref=gat.at[l, zh, me, pl.ds(*span)],
@@ -199,12 +193,12 @@
                 arrive(*at(unit, 2), span, half)
         add(*at(unit, 2))
 
-    def cross(unit, dx=0):
-        push(*at(unit, dx), WHOLE, across)
-
-    def crossed(unit):
-        arrive(*at(unit, 0), WHOLE)
-        spread(unit, WHOLE)
+    def cross(unit, dx=0, span=WHOLE):
+        push(*at(unit, dx), span, across)
+
+    def crossed(unit, span=WHOLE):
+        arrive(*at(unit, 0), span)
+        spread(unit, span)
 
     def take(unit, *steps):
         for dx in steps:
@@ -218,68 +212,82 @@
     send_to(0, B, 1)
     own_part(B)
     send_to(1, A, 0)
-    send_to(3, A, 0)
+    send_to(2, A, 0)
     receive(0, A, 0)
     spread(U[0], A)
     send_to(1, B, 1)
-    send_to(3, B, 1)
+    send_to(2, B, 1)
     receive(0, B, 1)
     spread(U[0], B)
     cross(U[0])
-    send_to(2, WHOLE, 0)
+    send_to(3, A, 0)
+    send_to(3, B, 1)
     added(U[0], 0)
     relay(U[0], A)
-    for n in (2, 1):
+    for n in (1, 2):
         receive(n, A, 0)
+        cross(U[n], 0, A)
         spread(U[n], A)
     relay(U[0], B)
     added(U[0], 3, 1)
-    for n in (2, 1):
+    for n in (1, 2):
         receive(n, B, 1)
-        cross(U[n])
+        cross(U[n], 0, B)
         spread(U[n], B)
         added(U[n], 0)
     for n in (2, 1):
         relay(U[n], A)
+    for n in (2, 1):
+        crossed(V[n], A)
     finish(U[0], A, B)
     for n in (2, 1):
         relay(U[n], B)
         added(U[n], 3, 1)
+    receive(3, A, 0)
+    cross(U[3], 0, A)
+    spread(U[3], A)
     for n in (2, 1):
-        crossed(V[n])
+        crossed(V[n], B)
         added(V[n], 0)
-    receive(3, WHOLE, 0)
-    cross(U[3])
-    spread(U[3], WHOLE)
+    receive(3, B, 1)
+    cross(U[3], 0, B)
+    spread(U[3], B)
     added(U[3], 0)
     cross(U[0], 1)
+    cross(U[0], 3)
     finish(U[2], A, B)
     cross(U[2], 2)
-    cross(U[0], 3)
     cross(U[0], 2)
     finish(U[1], A, B)
-    take(V[2], 3, 1)
-    relay(V[1], WHOLE)
+    crossed(V[3], A)
+    for n in (3, 1):
+        for span in PARTS:
+            arrive(*at(V[2], n), span)
+        add(*at(V[2], n))
+    relay(V[1], A)
+    relay(V[1], B)
     added(V[1], 3, 1)
-    crossed(V[3])
+    crossed(V[3], B)
     added(V[3], 0)
-    relay(U[3], WHOLE)
+    relay(U[3], A)
+    relay(V[3], A)
+    relay(U[3], B)
     added(U[3], 3, 1)
+    relay(V[3], B)
+    added(V[3], 3, 1)
     take(V[2], 2)
-    finish(V[1], WHOLE)
+    finish(V[1], A, B)
     take(V[0], 0, 1)
-    relay(V[3], WHOLE)
-    added(V[3], 3, 1)
-    finish(U[3], WHOLE)
+    finish(U[3], A, B)
     take(V[0], 3, 2)
-    finish(V[3], WHOLE)
+    finish(V[3], A, B)
     for p in range(2):
         wait_for(s1[p].at[pl.ds(0, NL - 1)], s1_send.at[p])
     wait_for(s2, s2_send)
     wait_for(gat.at[pl.ds(0, NL - 1)], g_send)
 
 
-ORDER = {0: 0, 1: SIDE - 1, 3: 2 * SIDE - 1, 2: 3 * SIDE - 1}
+FIRST = {0: 0, 2: SIDE - 1, 1: 2 * SIDE - 1, 3: 3 * SIDE - 1}
 
 
 def on_device(update, resident, placement, counts):
@@ -297,10 +305,11 @@
             *[pltpu.VMEM((NL, EXP, size, SLAB, LANE), bf16) for _ in range(2) for _, size in PARTS],
             pltpu.VMEM((NE - 1, TPD, SLAB, LANE), bf16),
             pltpu.VMEM((NL, NH, SIDE, TPD, SLAB, LANE), bf16),
+            pltpu.VMEM((1, NE), jnp.int32),
             pltpu.SMEM((NE,), jnp.int32),
-            pltpu.SMEM((NE,), jnp.int32),
-            pltpu.SMEM((NE,), jnp.int32),
-            dma((4,)),
+            pltpu.VMEM((NE, LANE), jnp.int32),
+            pltpu.SMEM((NE, LANE), jnp.int32),
+            dma((5,)),
             dma((2,)),
             dma((2,)),
             dma,
@@ -310,7 +319,7 @@
         ],
         compiler_params=pltpu.CompilerParams(collective_id=0, has_side_effects=True, vmem_limit_bytes=VMEM_LIMIT),
         name="refresh",
-    )(*(pltpu.with_memory_space_constraint(a, pltpu.HBM) for a in (update, resident.reshape(rows, cols), placement, counts)))
+    )(*(pltpu.with_memory_space_constraint(a, pltpu.HBM) for a in (update, resident.reshape(rows, cols), placement.reshape(1, NE), counts)))
     return result[None]
 
 

time: 65.4 us -> 65 us (level)
  no operation moved by 1% of the time
where the time goes in v5:
time: 65 us; the launch traced here: 64.9 us
  Pallas kernels  62.5 us (96%)
  local copies, waits for them, and re-layouts  2.36 us (4%)
    pallas_call x1, Pallas kernels, on_device(): pl.pallas_call(kernel, out_shape=pltpu.VMEM((rows, cols), bf16), in_specs...  62.5 us
    unnamed x1, local copies, waits for them, and re-layouts  2.36 us

profile of v5, /device:TPU:1, one launch (start us, length us, event | category | flops | bytes accessed | tf_op | source)
XLA Modules:
  0.0 64.9 jit_solution(3281046275205949060)
XLA Ops:
  0.0 62.5 %refresh.1 = bf16[2560,1024]{1,0:T(8,128)(2,1)S(1)} custom-call(f32[4,5,128,128]{3,2,1,0:T(8,128)} %update.1, bf16[2560,1024]{1,0:T(8,128)(2,1)} %bitcast.4, s32[1,32]{1,0:T(1,128)} %bitcast.5, s32[32]{0:T(128)} %counts_in.1), custom_call_target="tpu_custom_call" | custom-call | tf_op jit(solution)/shard_map/refresh/pallas_call | solution.py:297
  62.6 2.4 %copy.6 = bf16[1,2560,1024]{2,1,0:T(8,128)(2,1)} copy(bf16[1,2560,1024]{2,1,0:T(8,128)(2,1)S(1)} %bitcast.3) | data formatting | bytes 10485760

commit v6 on v5

--- a/solution.py
+++ b/solution.py
@@ -290,6 +290,21 @@
 FIRST = {0: 0, 2: SIDE - 1, 1: 2 * SIDE - 1, 3: 3 * SIDE - 1}
 
 
+STORES = 8
+
+
+def store(held, out, sem):
+    size = held.shape[0] // STORES
+    copies = []
+    for n in range(STORES):
+        rows = pl.ds(n * size, size)
+        cp = pltpu.make_async_copy(held.at[rows], out.at[rows], sem.at[n])
+        cp.start()
+        copies.append(cp)
+    for cp in copies:
+        cp.wait()
+
+
 def on_device(update, resident, placement, counts):
     _, rows, cols = resident.shape
     bf16 = jnp.bfloat16
@@ -320,7 +335,16 @@
         compiler_params=pltpu.CompilerParams(collective_id=0, has_side_effects=True, vmem_limit_bytes=VMEM_LIMIT),
         name="refresh",
     )(*(pltpu.with_memory_space_constraint(a, pltpu.HBM) for a in (update, resident.reshape(rows, cols), placement.reshape(1, NE), counts)))
-    return result[None]
+    final = pl.pallas_call(
+        store,
+        out_shape=pltpu.HBM((rows, cols), bf16),
+        in_specs=[pl.BlockSpec(memory_space=pltpu.VMEM)],
+        out_specs=pl.BlockSpec(memory_space=pltpu.HBM),
+        scratch_shapes=[dma((STORES,))],
+        compiler_params=pltpu.CompilerParams(vmem_limit_bytes=16 << 20),
+        name="store",
+    )(pltpu.with_memory_space_constraint(result, pltpu.VMEM))
+    return final[None]
 
 
 def solution(mesh):

time: 65 us -> 65 us (level)
  Pallas kernels: 62.5 us -> 65 us
  local copies, waits for them, and re-layouts: 2.36 us -> 0 us
    pallas_call x0 -> x1, Pallas kernels: none -> 2.42 us  [on_device(): pl.pallas_call(store, out_shape=pltpu.HBM((rows, cols), bf16), in_specs=[...]
    unnamed x1 -> x0, local copies, waits for them, and re-layouts: 2.36 us -> none
where the time goes in v6:
time: 65 us
  Pallas kernels  65 us (100%)
    pallas_call x1, Pallas kernels, on_device(): pl.pallas_call(kernel, out_shape=pltpu.VMEM((rows, cols), bf16), in_specs...  62.5 us
    pallas_call x1, Pallas kernels, on_device(): pl.pallas_call(store, out_shape=pltpu.HBM((rows, cols), bf16), in_specs=[...  2.42 us

profile of v6, /device:TPU:1, one launch (start us, length us, event | category | flops | bytes accessed | tf_op | source)
XLA Modules:
  0.0 65.0 jit_solution(1846074539995358835)
XLA Ops:
  0.0 62.5 %refresh.1.held = bf16[2560,1024]{1,0:T(8,128)(2,1)S(1)} custom-call(f32[4,5,128,128]{3,2,1,0:T(8,128)} %update.1, bf16[2560,1024]{1,0:T(8,128)(2,1)} %bitcast.3, s32[1,32]{1,0:T(1,128)} %bitcast.4, s32[32]{0:T(128)} %counts_in.1), custom_call_target="tpu_custom_call" | custom-call | tf_op jit(solution)/shard_map/refresh/pallas_call | solution.py:312
  62.6 2.4 %store.1 = bf16[2560,1024]{1,0:T(8,128)(2,1)} custom-call(bf16[2560,1024]{1,0:T(8,128)(2,1)S(1)} %refresh.1.held), custom_call_target="tpu_custom_call" | custom-call | tf_op jit(solution)/shard_map/store/pallas_call | solution.py:338
